TPU v7x, 512 devices: a whole 4x4x16 slice. The times are simulated.
512 devices in a mesh: tm: 128 (over z, y, core), lev: 4 (over x).
Axes of the slice: x: 4, y: 4, z: 16, core: 2. Of those that a mesh axis runs over, the one named last changes fastest.
Arguments:
- field: bfloat16 [256, 4, 384, 384], P('tm', 'lev'), may hold values from -6 to 6
- patch_list: int32 [128, 128, 2], P('tm'), may hold values from -1 to 31, as said below
- track_time: int32 [4096], replicated, may hold values from 0 to 255
- track_row: int32 [4096], replicated, may hold values from 64 to 320
- track_col: int32 [4096], replicated, may hold values from 64 to 320
Outputs:
- point_fields: bfloat16 [4096, 4, 512], P('tm', 'lev')
- composite: float32 [4, 512], P('lev')
- covariance: float32 [128, 128], P('lev')
Inputs may be any that keep to these rules, and one draw needn't show every extreme that they name: For each owner d, each k appears at most once in patch_list[:, d, :]; where patch_list[s, d, c] = k >= 0, track_time[d * 32 + k] lies in group s, that is from s * 2 to (s + 1) * 2 - 1; some group fills all 2 slots to some owner.
All inputs are finite; a program needn't handle non-finite values.
Results may differ from a plain program's by a relative error of at most 0.001.
Values may be sent and summed in bfloat16 or wider, within the bound.
A program may use at most 64 MiB of HBM per device.

v0:
```python
import math

import jax
import jax.numpy as jnp
from jax import lax
from jax.sharding import PartitionSpec as P

PATCH = 128
NR = 32
NA = 16


def polar_offsets(patch, radii, azimuths):
    cycle = jnp.arange(radii, dtype=jnp.float32)
    turn = jnp.arange(azimuths, dtype=jnp.float32)
    radius = (cycle[:, None] + 1.0) * (5.0 * patch / (16.0 * radii))
    theta = turn[None, :] * (2.0 * math.pi / azimuths)
    across = (radius * jnp.cos(theta)).reshape(-1)
    along = (radius * jnp.sin(theta)).reshape(-1)
    return (across, along)


def row_weights(along, patch):
    row_pos = 0.5 * patch + along
    lower = jnp.floor(row_pos)
    frac = row_pos - lower
    lower = lower.astype(jnp.int32)
    cells = jnp.arange(patch, dtype=jnp.int32)[None, :]
    table = jnp.where(cells == lower[:, None], 1.0 - frac[:, None], 0.0) + jnp.where(
        cells == lower[:, None] + 1, frac[:, None], 0.0
    )
    return table.astype(jnp.bfloat16)


def regrid(frames, centre_rows, height):
    count, patch = (frames.shape[0], frames.shape[1])
    across, along = polar_offsets(patch, NR, NA)
    weights_rows = row_weights(along, patch)
    block = math.gcd(count, 16)
    cells = jnp.arange(patch, dtype=jnp.int32)

    def one_block(item):
        tiles, local_rows = item
        mixed = jnp.einsum("pi,bij->bpj", weights_rows, tiles, preferred_element_type=jnp.float32)
        latitude = 0.25 * (0.5 * (height - 1) - local_rows.astype(jnp.float32))
        coslat = jnp.cos(latitude * (math.pi / 180.0))
        col_pos = 0.5 * patch + across[None, :] / coslat[:, None]
        lower = jnp.floor(col_pos)
        frac = (col_pos - lower)[..., None]
        lower = lower.astype(jnp.int32)[..., None]
        weights_cols = jnp.where(cells == lower, 1.0 - frac, 0.0) + jnp.where(
            cells == lower + 1, frac, 0.0
        )
        return jnp.sum(mixed * weights_cols, axis=-1)

    result = lax.map(
        one_block,
        (
            frames.reshape(count // block, block, patch, patch),
            centre_rows.reshape(count // block, block),
        ),
    )
    return result.reshape(count, -1)


def placement(received_ids, points_dev):
    flat = received_ids.reshape(-1)
    match = flat[None, :] == jnp.arange(points_dev, dtype=jnp.int32)[:, None]
    slot = jnp.sum(jnp.where(match, jnp.arange(flat.shape[0], dtype=jnp.int32)[None, :], 0), axis=1)
    return (slot, jnp.any(match, axis=1))


def body(field, patch_list, track_time, track_row, track_col):
    tm_count = lax.axis_size("tm")
    here = lax.axis_index("tm")
    times_dev, levels_dev, height, width = field.shape
    points_dev = track_time.shape[0] // tm_count
    half = PATCH // 2
    targets = patch_list[0]
    capacity = targets.shape[1]
    live = targets >= 0
    owner = jnp.arange(tm_count, dtype=jnp.int32)[:, None]
    point = (owner * points_dev + jnp.maximum(targets, 0)).reshape(-1)
    local_time = jnp.clip(jnp.take(track_time, point) - here * times_dev, 0, times_dev - 1)
    rows_sent = jnp.take(track_row, point)
    cols_sent = jnp.take(track_col, point)
    anchor = jnp.zeros((), jnp.int32)

    def cut(time_index, row, col):
        return lax.dynamic_slice(
            field, (time_index, anchor, row - half, col - half), (1, levels_dev, PATCH, PATCH)
        )[0]

    frames = jax.vmap(cut)(local_time, rows_sent, cols_sent)
    frames = jnp.where(live.reshape(-1)[:, None, None, None], frames, jnp.zeros((), jnp.bfloat16))
    owned_rows = lax.dynamic_slice_in_dim(track_row, here * points_dev, points_dev)
    sent = frames.reshape(tm_count, capacity, levels_dev, PATCH, PATCH)
    received_frames, got_ids = (
        lax.all_to_all(sent, "tm", split_axis=0, concat_axis=0, tiled=True),
        lax.all_to_all(targets, "tm", split_axis=0, concat_axis=0, tiled=True),
    )
    slot, present = placement(got_ids, points_dev)
    chosen = jnp.take(received_frames.reshape(-1, levels_dev, PATCH, PATCH), slot, axis=0)
    chosen = jnp.where(present[:, None, None, None], chosen, jnp.zeros((), jnp.bfloat16))
    polar = regrid(chosen.reshape(-1, PATCH, PATCH), jnp.repeat(owned_rows, levels_dev), height)
    polar = polar.reshape(points_dev, levels_dev, -1)
    count = jnp.sum(present.astype(jnp.float32))
    profile = jnp.mean(polar.reshape(points_dev, levels_dev, NR, NA), axis=-1)
    whole = lax.all_gather(profile, "lev", axis=1, tiled=True).reshape(points_dev, -1)
    mine = profile.reshape(points_dev, -1)
    gram_rows = jnp.dot(
        mine.T, whole, precision=lax.Precision.HIGHEST, preferred_element_type=jnp.float32
    )
    polar_sum, gram_sum, profile_sum, total = lax.psum(
        (jnp.sum(polar, axis=0), gram_rows, jnp.sum(whole, axis=0), count), "tm"
    )
    composite = polar_sum / total
    mean_all = profile_sum / total
    span = mine.shape[1]
    mean_mine = lax.dynamic_slice_in_dim(mean_all, lax.axis_index("lev") * span, span)
    covariance = gram_sum / total - mean_mine[:, None] * mean_all[None, :]
    return (polar.astype(jnp.bfloat16), composite, covariance)


def solution(mesh):
    placed = (P("tm", "lev", None, None), P("tm", None, None), P(), P(), P())
    return jax.shard_map(
        body,
        mesh=mesh,
        in_specs=placed,
        out_specs=(P("tm", "lev", None), P("lev", None), P("lev", None)),
        check_vma=False,
    )
```

profile of v0, /device:TPU:1, one launch (start us, length us, event | category | flops | bytes accessed | tf_op | source)
XLA Modules:
  0.0 1997.1 jit_solution(3538341386044115729)
XLA Ops:
  2.1 20.6 %all-to-all-start = ((s32[128,1,2]{2,1,0:T(1,128)}), s32[128,1,2]{2,1,0:T(1,128)S(1)}, u32[]{:S(2)}, u32[]{:S(2)}) async-start(s32[128,1,2]{2,1,0:T(1,128)} %bitcast), calls=%async_computation | async-start | bytes 131072 | tf_op jit(solution)/shard_map/all_to_all | solution.py:100
  30.3 1062.0 %while.15 = (s32[]{:T(128)}, bf16[2,1,384,384]{3,2,1,0:T(8,128)(2,1)}, s32[256,4]{0,1:T(4,128)S(1)}, bf16[256,1,1,128,128]{4,3,2,1,0:T(8,128)(2,1)}, s32[]{:T(128)}) while((s32[]{:T(128)}, bf16[2,1,384,384]{3,2,1,0:T(8,128)(2,1)}, s32[256,4]{0,1:T(4,128)S(1)}, bf16[256,1,1,128,128]{4,3,2,1,0:T(8,128)(2,1)}, s32[]{:T(128)}) %tuple.61), condition=%wide.while_cond, body=%wide.while_body.sunk | while | flops 2 | bytes 67705 | solution.py:90
  35.1 3.5 bitcast_dynamic-update-slice_fusion.4
  201.0 3.5 bitcast_dynamic-update-slice_fusion.4
  213.5 3.5 bitcast_dynamic-update-slice_fusion.4
  271.6 3.5 bitcast_dynamic-update-slice_fusion.4
  375.3 3.5 bitcast_dynamic-update-slice_fusion.4
  387.7 3.5 bitcast_dynamic-update-slice_fusion.4
  553.6 3.5 bitcast_dynamic-update-slice_fusion.4
  624.2 3.5 bitcast_dynamic-update-slice_fusion.4
  686.4 3.5 bitcast_dynamic-update-slice_fusion.4
  703.0 3.5 bitcast_dynamic-update-slice_fusion.4
  723.8 3.5 bitcast_dynamic-update-slice_fusion.4
  848.2 3.5 bitcast_dynamic-update-slice_fusion.4
  856.5 3.5 bitcast_dynamic-update-slice_fusion.4
  947.8 3.5 bitcast_dynamic-update-slice_fusion.4
  1047.4 3.5 bitcast_dynamic-update-slice_fusion.4
  1092.5 7.3 broadcast_select_fusion
  1099.7 16.6 all-to-all-start.1
  1120.0 361.2 %all-to-all-done.1 = bf16[128,2,1,128,128]{4,3,1,2,0:T(8,128)(2,1)} async-done(((bf16[128,2,1,128,128]{4,3,1,2,0:T(8,128)(2,1)}), bf16[128,2,1,128,128]{4,3,1,2,0:T(8,128)(2,1)}, u32[]{:S(2)}, u32[]{:S(2)}) %all-to-all-start.1) | async-done | bytes 8388640 | tf_op jit(solution)/shard_map/all_to_all | solution.py:99
  1481.2 4.1 gather_fusion
  1486.2 4.7 while.16
  1491.4 9.3 all-gather
  1501.7 491.9 %all-reduce = (f32[1,512]{1,0:T(1,128)S(1)}, f32[]{:T(128)}, f32[32,128]{1,0:T(8,128)S(1)}, f32[128]{0:T(128)S(1)}) all-reduce(f32[1,512]{1,0:T(1,128)S(1)} %bitcast.57, f32[]{:T(128)} %convert_reduce_fusion, f32[32,128]{1,0:T(8,128)S(1)} %fusion.26, f32[128]{0:T(128)S(1)} %reduce.4), channel_id=1, replica_groups=mesh['tm'=128,'lev'=4] {'tm'}, use_global_device_ids=true, to_apply=%region_6.8 | all-reduce | flops 4737 | bytes 37896 | tf_op jit(solution)/shard_map/psum | solution.py:114
  (822 shorter events, 1032.4 us)
Async XLA Ops:
  0.6 23.9 %copy-start = (s32[4096]{0:T(1024)S(1)}, s32[4096]{0:T(1024)}, u32[]{:S(2)}) copy-start(s32[4096]{0:T(1024)} %param.11) | copy-start | bytes 49156
  2.1 1097.7 %all-to-all-start = ((s32[128,1,2]{2,1,0:T(1,128)}), s32[128,1,2]{2,1,0:T(1,128)S(1)}, u32[]{:S(2)}, u32[]{:S(2)}) async-start(s32[128,1,2]{2,1,0:T(1,128)} %bitcast), calls=%async_computation | async-start | bytes 131072 | tf_op jit(solution)/shard_map/all_to_all | solution.py:100
  1099.7 381.4 %all-to-all-start.1 = ((bf16[128,2,1,128,128]{4,3,1,2,0:T(8,128)(2,1)}), bf16[128,2,1,128,128]{4,3,1,2,0:T(8,128)(2,1)}, u32[]{:S(2)}, u32[]{:S(2)}) async-start(bf16[128,2,1,128,128]{4,3,1,2,0:T(8,128)(2,1)} %broadcast_select_fusion), calls=%async_computation.1 | async-start | bytes 16777216 | tf_op jit(solution)/shard_map/all_to_all | solution.py:99
where the time goes:
time: 2020 us; the launch traced here: 2000 us
  local copies, waits for them, and re-layouts  1080 us (53%)
  blocking collectives  501 us (25%)
  waiting for transfers between devices  361 us (18%)
  starting transfers between devices  37.1 us (2%)
    gather x768, local copies, waits for them, and re-layouts  1060 us
    psum x1, blocking collectives, body(): lax.psum((jnp.sum(polar, axis=0), gram_rows, jnp.sum(whole, axis=0), coun...  492 us
    all_to_all x1, waiting for transfers between devices, body(): lax.all_to_all(sent, 'tm', split_axis=0, concat_axis=0, tiled=True)  361 us
  transfers between devices with their start and end apart: 2, of which 1 were waited for; matrix products, arithmetic and copies ran while one was open for 54% of the time, Pallas kernels for 0%

commit v1 on v0

v1 whole, which is shorter than its diff:
```python
import functools
import math

import jax
import jax.numpy as jnp
import numpy as np
from jax import lax
from jax.experimental import pallas as pl
from jax.experimental.pallas import tpu as pltpu
from jax.sharding import PartitionSpec as P

PATCH, NR, NA = 128, 32, 16
HALF = PATCH // 2
SIZE = 384
POINTS_DEV = 32
OWNERS, SLOTS = 128, 2
PLANES, MATES, LEVS = 16, 8, 4
SPAN = 64
TILES = ((0, 6), (4, 8), (0, 3), (1, 8))
GROUPS = 4
CHUNKS = 5


def tables():
    with jax.ensure_compile_time_eval():
        cycle = jnp.arange(NR, dtype=jnp.float32)
        turn = jnp.arange(NA, dtype=jnp.float32)
        radius = (cycle[:, None] + 1.0) * (5.0 * PATCH / (16.0 * NR))
        theta = turn[None, :] * (2.0 * math.pi / NA)
        across = np.asarray((radius * jnp.cos(theta)).reshape(-1))
        along = (radius * jnp.sin(theta)).reshape(-1)
        pos = 0.5 * PATCH + along
        low = jnp.floor(pos)
        frac = pos - low
        upper = np.asarray(frac.astype(jnp.bfloat16)).astype(np.float32)
        lower = np.asarray((1.0 - frac).astype(jnp.bfloat16)).astype(np.float32)
        low = np.asarray(low.astype(jnp.int32))
        latitude = 0.25 * (0.5 * (SIZE - 1) - jnp.arange(SIZE, dtype=jnp.float32))
        stretch = np.asarray(1.0 / jnp.cos(latitude * (math.pi / 180.0)))
    turns = np.arange(NR * NA) % NA
    key = np.where(turns == NA // 4, -1e-3, np.where(turns == 3 * NA // 4, 1e-3, across))
    order = np.argsort(key, kind="stable")
    q = np.arange(NR * NA)
    weights = np.zeros((PATCH, NR * NA), np.float32)
    weights[low[order], q] += lower[order]
    weights[low[order] + 1, q] += upper[order]
    mean = np.zeros((4, NR, 128), np.float32)
    mean[q // 128, order // NA, q % 128] = 1.0 / NA
    unsort = np.zeros((NR * NA, NR * NA), np.float32)
    unsort[q, order] = 1.0
    spread = np.ascontiguousarray(np.broadcast_to(across[order].reshape(4, 1, 128), (4, 8, 128)), np.float32)
    return stretch, weights.astype(jnp.bfloat16), spread, mean, unsort.astype(jnp.bfloat16)


def merge(a, b, step, mask):
    if step == 4:
        return jnp.where(mask, a, b) + pltpu.roll(jnp.where(mask, b, a), 4, 0)
    return jnp.where(mask, a + pltpu.roll(a, 8 - step, 0), b + pltpu.roll(b, step, 0))


def regrid_kernel(
    list_ref, time_ref, row_ref, col_ref, stretch_ref, field_ref, weights_ref, across_ref, mean_ref,
    send_ref, prof_ref, sums_ref, turned, polar,
):
    here = lax.axis_index("tm")
    for t in range(2):
        for i in range(3):
            for j in range(3):
                tile = field_ref[t, 0, i * 128 : (i + 1) * 128, j * 128 : (j + 1) * 128]
                turned[t, i, j * 128 : (j + 1) * 128, :] = tile.astype(jnp.float32).T
    sub = lax.broadcasted_iota(jnp.int32, (8, 128), 0)
    first = (lax.broadcasted_iota(jnp.int32, (8, 128), 1) & 4) == 0
    lane = lax.broadcasted_iota(jnp.int32, (SPAN, 128), 1)
    subf = sub.astype(jnp.float32)
    m4, m2, m1 = sub < 4, (sub & 2) == 0, (sub & 1) == 0

    def plane(g, carry):
        total, count = carry
        halves, info = ([], []), []
        names = jnp.zeros((8, 128), jnp.int32)
        for o in range(MATES):
            owner = g * MATES + o
            ids = []
            for p in range(SLOTS):
                k = list_ref[owner * SLOTS + p]
                ids.append(k)
                point = owner * POINTS_DEV + jnp.maximum(k, 0)
                t = jnp.clip(time_ref[point] - 2 * here, 0, 1)
                row, col = row_ref[point], col_ref[point]
                top = row - HALF
                b = jnp.minimum(top // 128, 1)
                off = top - b * 128
                starts = [pl.multiple_of((col - reach) // 8 * 8, 8) for reach in (48, 1)]
                for h in range(2):
                    one = turned[t, b, pl.ds(starts[h], SPAN), :]
                    two = turned[t, b + 1, pl.ds(starts[h], SPAN), :]
                    both = jnp.where(lane >= off, one, two)
                    halves[h].append(pltpu.roll(both, 128 - off, 1).astype(jnp.bfloat16))
                live = jnp.where(k >= 0, 1.0, 0.0)
                count += live
                info.append((stretch_ref[row], [(col - s).astype(jnp.float32) for s in starts], live))
            names = jnp.where(sub == o, jnp.where(first, ids[0], ids[1]), names)
        mixed = [
            jnp.dot(
                jnp.concatenate(halves[h], 0),
                weights_ref[:, h * 256 : (h + 1) * 256],
                preferred_element_type=jnp.float32,
            )
            for h in range(2)
        ]
        for o in range(MATES):
            accs = []
            for n in (2 * o, 2 * o + 1):
                s, centre, _ = info[n]
                for blk in range(4):
                    base = across_ref[blk] * s + (centre[blk // 2] - subf)
                    acc = None
                    for tile in range(*TILES[blk]):
                        w = jnp.maximum(1.0 - jnp.abs(base - 8.0 * tile), 0.0)
                        at = n * SPAN + tile * 8
                        v = mixed[blk // 2][at : at + 8, (blk % 2) * 128 : (blk % 2 + 1) * 128]
                        acc = w * v if acc is None else acc + w * v
                    accs.append(acc)
            a = [accs[i] for i in (0, 4, 2, 6, 1, 5, 3, 7)]
            a = [merge(a[i], a[i + 1], 4, m4) for i in (0, 2, 4, 6)]
            a = [merge(a[i], a[i + 1], 2, m2) for i in (0, 2)]
            out = merge(a[0], a[1], 1, m1) * jnp.where(m4, info[2 * o][2], info[2 * o + 1][2])
            polar[pl.ds(pl.multiple_of((g * MATES + o) * 8, 8), 8), :] = out
            send_ref[g, o] = out.astype(jnp.bfloat16)
            total = total + out
        send_ref[g, MATES] = names.astype(jnp.float32).astype(jnp.bfloat16)
        return total, count

    total, count = lax.fori_loop(0, PLANES, plane, (jnp.zeros((8, 128), jnp.float32), 0.0))
    sums_ref[...] = jnp.where(m4, jnp.where(sub == 1, count, 0.0), total + pltpu.roll(total, 4, 0))
    acc = jnp.zeros((NR, OWNERS * SLOTS), jnp.float32)
    for b in range(4):
        acc += lax.dot_general(
            mean_ref[b], polar[pl.ds(b, OWNERS * SLOTS, stride=4), :], (((1,), (1,)), ((), ())),
            precision=lax.Precision.HIGHEST, preferred_element_type=jnp.float32,
        )
    prof_ref[...] = acc


def exchange_kernel(
    send_ref, prof_ref, sums_ref, unsort_ref, out_ref, comp_ref, cov_ref,
    planes, mates, names, named, profs, part, red1, red2, red3, mine,
    plane_s, plane_r, mate_s, mate_r, name_s, name_r, prof_s, prof_r, r1_s, r1_r, r2_s, r2_r, r3_s, r3_r,
):
    tm, lev = lax.axis_index("tm"), lax.axis_index("lev")
    z, yc = tm // MATES, lax.rem(tm, MATES)
    PER = PLANES // GROUPS

    def plane_peer(d):
        return {"tm": lax.rem(z + d, PLANES) * MATES + yc}

    def mate_peer(d):
        return {"tm": z * MATES + lax.rem(yc + d, MATES)}

    def lev_peer(d):
        return {"lev": lax.rem(lev + d, LEVS)}

    def copy(src, dst, s, r, peer):
        return pltpu.make_async_remote_copy(
            src_ref=src, dst_ref=dst, send_sem=s, recv_sem=r, device_id=peer, device_id_type=pl.DeviceIdType.MESH
        )

    def each(n, f):
        def step(i, c):
            f(i)
            return c

        lax.fori_loop(1, n, step, 0)

    barrier = pltpu.get_barrier_semaphore()

    def greet(peer):
        pl.semaphore_signal(barrier, inc=1, device_id=peer, device_id_type=pl.DeviceIdType.MESH)

    each(LEVS, lambda d: greet(lev_peer(d)))
    each(MATES, lambda d: greet(mate_peer(d)))
    each(PLANES, lambda d: greet(plane_peer(d)))
    pl.semaphore_wait(barrier, LEVS + MATES + PLANES - 3)

    def prof_copy(d):
        return copy(prof_ref, profs.at[d], prof_s.at[d], prof_r.at[d], lev_peer(d))

    def plane_copy(d):
        there = lax.rem(z + d, PLANES)
        return copy(send_ref.at[there], planes.at[d], plane_s.at[d], plane_r.at[d], plane_peer(d))

    def mate_copy(g, d):
        there = lax.rem(yc + d, MATES)
        return copy(
            planes.at[pl.ds(g * PER, PER), there], mates.at[d, pl.ds(g * PER, PER)],
            mate_s.at[g, d], mate_r.at[g, d], mate_peer(d),
        )

    def name_copy(d):
        return copy(names, named.at[d], name_s.at[d], name_r.at[d], mate_peer(d))

    each(LEVS, lambda d: prof_copy(d).start())
    each(PLANES, lambda d: plane_copy(d).start())
    planes[0] = send_ref[z]
    profs[0] = prof_ref[...]

    each(LEVS, lambda d: prof_copy(d).wait_recv())
    whole = jnp.concatenate([profs[lax.rem(lev - l + LEVS, LEVS)] for l in range(LEVS)], 0)
    both = lax.dot_general(
        jnp.concatenate([prof_ref[...], jnp.ones((8, OWNERS * SLOTS), jnp.float32)], 0), whole, (((1,), (1,)), ((), ())),
        precision=lax.Precision.HIGHEST, preferred_element_type=jnp.float32,
    )
    for c in range(4):
        part[c] = both[c * 8 : (c + 1) * 8]
    sub = lax.broadcasted_iota(jnp.int32, (8, 128), 0)
    part[4] = jnp.where(sub == 0, both[32:40], sums_ref[...])

    def r1_copy(c):
        d = lax.rem(c - yc + MATES, MATES)
        return copy(part.at[c], red1.at[d], r1_s.at[c], r1_r.at[d], {"tm": z * MATES + c})

    def r2_copy(d):
        return copy(mine.at[0], red2.at[d], r2_s.at[d], r2_r.at[d], plane_peer(d))

    def r3_copy(d):
        return copy(mine.at[1], red3.at[yc], r3_s.at[d], r3_r.at[yc], mate_peer(d))

    def r1_each(f):
        for c in range(CHUNKS):
            @pl.when(yc != c)
            def _():
                f(c)

    def pass_on(g):
        for d in range(g * PER, (g + 1) * PER):
            if d:
                plane_copy(d).wait_recv()
        each(MATES, lambda d: mate_copy(g, d).start())

    r1_each(lambda c: r1_copy(c).start())
    pass_on(0)

    @pl.when(yc < CHUNKS)
    def _():
        def arrived(d):
            return copy(part.at[0], red1.at[d], r1_s.at[0], r1_r.at[d], mate_peer(1))

        each(MATES, lambda d: arrived(d).wait_recv())
        red1[0] = part[yc]
        total = red1[lax.rem(yc, MATES)]
        for m in range(1, MATES):
            total += red1[lax.rem(yc - m + MATES, MATES)]
        mine[0] = total
        each(PLANES, lambda d: r2_copy(d).start())

    pass_on(1)

    @pl.when(yc < CHUNKS)
    def _():
        each(PLANES, lambda d: r2_copy(d).wait_recv())
        red2[0] = mine[0]
        total = red2[lax.rem(z, PLANES)]
        for m in range(1, PLANES):
            total += red2[lax.rem(z - m + PLANES, PLANES)]
        mine[1] = total
        red3[yc] = total
        each(MATES, lambda d: r3_copy(d).start())

    pass_on(2)
    pass_on(3)

    lane = lax.broadcasted_iota(jnp.int32, (8, 128), 1)
    ids = jnp.zeros((8, 128), jnp.float32)
    for d in range(PLANES):
        ids = jnp.where(lane // 8 == d, planes[d, MATES].astype(jnp.float32), ids)
    names[...] = ids
    each(MATES, lambda d: name_copy(d).start())

    for c in range(CHUNKS):
        @pl.when(yc != c)
        def _():
            copy(mine.at[1], red3.at[c], r3_s.at[0], r3_r.at[c], mate_peer(1)).wait_recv()

    count = red3[4, 1:2, :]
    every = red3[4, 0:1, :] / count
    row = lax.broadcasted_iota(jnp.int32, (NR, 128), 0)
    column = lax.broadcasted_iota(jnp.int32, (NR, 128), 1)
    own = jnp.sum(jnp.where(column == lev * NR + row, every, 0.0), axis=1, keepdims=True)
    gram = jnp.concatenate([red3[c] for c in range(4)], 0)
    cov_ref[...] = gram / count - own * every
    comp = red3[4, 4:8, :] / count
    comp = jnp.concatenate([comp[b : b + 1] for b in range(4)], 1)
    high = comp.astype(jnp.bfloat16).astype(jnp.float32)
    middle = (comp - high).astype(jnp.bfloat16).astype(jnp.float32)
    terms = jnp.concatenate([high, middle, comp - high - middle], 0).astype(jnp.bfloat16)
    terms = jnp.dot(terms, unsort_ref[...], preferred_element_type=jnp.float32)
    comp_ref[...] = terms[0:1] + terms[1:2] + terms[2:3]

    named[0] = names[...]
    mates[0] = planes[:, yc]
    line = lax.broadcasted_iota(jnp.int32, (128, 128), 0)
    lane = lax.broadcasted_iota(jnp.int32, (128, 128), 1)
    wanted = jnp.where(lane % 4 == line // POINTS_DEV, line % POINTS_DEV, -9).astype(jnp.float32)
    each(MATES, lambda d: name_copy(d).wait_recv())
    picked = jnp.zeros((128, 128), jnp.float32)
    for g in range(GROUPS):
        each(MATES, lambda d: mate_copy(g, d).wait_recv())
    for d in range(MATES):
        hit = jnp.where(wanted == named[d, pl.ds(yc, 1), :], 1.0, 0.0).astype(jnp.bfloat16)
        rows = mates[d].astype(jnp.float32).reshape(128, 128).astype(jnp.bfloat16)
        picked += jnp.dot(hit, rows, preferred_element_type=jnp.float32)
    wide = jnp.concatenate([picked[b * POINTS_DEV : (b + 1) * POINTS_DEV] for b in range(4)], 1).astype(jnp.bfloat16)
    out_ref[...] = jnp.dot(wide, unsort_ref[...], preferred_element_type=jnp.float32).astype(jnp.bfloat16)

    each(LEVS, lambda d: prof_copy(d).wait_send())
    each(PLANES, lambda d: plane_copy(d).wait_send())
    each(MATES, lambda d: name_copy(d).wait_send())
    for g in range(GROUPS):
        each(MATES, lambda d: mate_copy(g, d).wait_send())
    r1_each(lambda c: r1_copy(c).wait_send())

    @pl.when(yc < CHUNKS)
    def _():
        each(PLANES, lambda d: r2_copy(d).wait_send())
        each(MATES, lambda d: r3_copy(d).wait_send())


def body(field, patch_list, track_time, track_row, track_col):
    stretch, weights, across, mean, unsort = tables()
    smem = pl.BlockSpec(memory_space=pltpu.SMEM)
    vmem = pl.BlockSpec(memory_space=pltpu.VMEM)
    f32, bf16 = jnp.float32, jnp.bfloat16
    send, prof, sums = pl.pallas_call(
        regrid_kernel,
        out_shape=(
            jax.ShapeDtypeStruct((PLANES, MATES + 1, 8, 128), bf16),
            jax.ShapeDtypeStruct((NR, OWNERS * SLOTS), f32),
            jax.ShapeDtypeStruct((8, 128), f32),
        ),
        in_specs=[smem] * 5 + [vmem] * 4,
        out_specs=(vmem,) * 3,
        scratch_shapes=[pltpu.VMEM((2, 3, SIZE, 128), f32), pltpu.VMEM((OWNERS * 8, 128), f32)],
        compiler_params=pltpu.CompilerParams(vmem_limit_bytes=40 << 20),
        name="regrid",
    )(
        patch_list.reshape(-1), track_time, track_row, track_col, jnp.asarray(stretch),
        field, jnp.asarray(weights), jnp.asarray(across), jnp.asarray(mean),
    )
    dma = pltpu.SemaphoreType.DMA
    out, comp, cov = pl.pallas_call(
        exchange_kernel,
        out_shape=(
            jax.ShapeDtypeStruct((POINTS_DEV, NR * NA), bf16),
            jax.ShapeDtypeStruct((1, NR * NA), f32),
            jax.ShapeDtypeStruct((NR, 128), f32),
        ),
        in_specs=[vmem] * 4,
        out_specs=(vmem,) * 3,
        scratch_shapes=[
            pltpu.VMEM((PLANES, MATES + 1, 8, 128), bf16),
            pltpu.VMEM((MATES, PLANES, 8, 128), bf16),
            pltpu.VMEM((8, 128), f32),
            pltpu.VMEM((MATES, 8, 128), f32),
            pltpu.VMEM((LEVS, NR, OWNERS * SLOTS), f32),
            pltpu.VMEM((CHUNKS, 8, 128), f32),
            pltpu.VMEM((MATES, 8, 128), f32),
            pltpu.VMEM((PLANES, 8, 128), f32),
            pltpu.VMEM((MATES, 8, 128), f32),
            pltpu.VMEM((2, 8, 128), f32),
            dma((PLANES,)), dma((PLANES,)), dma((GROUPS, MATES)), dma((GROUPS, MATES)), dma((MATES,)), dma((MATES,)),
            dma((LEVS,)), dma((LEVS,)), dma((MATES,)), dma((MATES,)), dma((PLANES,)), dma((PLANES,)),
            dma((MATES,)), dma((MATES,)),
        ],
        compiler_params=pltpu.CompilerParams(collective_id=0, has_side_effects=True, vmem_limit_bytes=40 << 20),
        name="exchange",
    )(send, prof, sums, jnp.asarray(unsort))
    return out[:, None, :], comp, cov


def solution(mesh):
    return jax.shard_map(
        body,
        mesh=mesh,
        in_specs=(P("tm", "lev", None, None), P("tm", None, None), P(), P(), P()),
        out_specs=(P("tm", "lev", None), P("lev", None), P("lev", None)),
        check_vma=False,
    )
```

time: 2020 us -> 64.6 us (0.03); the launches traced: 2000 us -> 64.1 us
  local copies, waits for them, and re-layouts: 1080 us -> 8.08 us
  blocking collectives: 501 us -> 0 us
  waiting for transfers between devices: 361 us -> 0 us
  Pallas kernels: 0 us -> 55.3 us
  starting transfers between devices: 37.1 us -> 0 us
    gather x773 -> x0, local copies, waits for them, and re-layouts: 1070 us -> none
    psum x1 -> x0, blocking collectives: 492 us -> none  [body(): lax.psum((jnp.sum(polar, axis=0), gram_rows, jnp.sum(whole, axis=0), coun...]
    all_to_all x2 -> x0, waiting for transfers between devices: 361 us -> none  [the longest x1 361 us: body(): lax.all_to_all(sent, 'tm', split_axis=0, concat_axis=0, tiled=True)]
    pallas_call x0 -> x2, Pallas kernels: none -> 55.3 us  [the longest x1 42.3 us: body(): pl.pallas_call(exchange_kernel, out_shape=(jax.ShapeDtypeStruct((POINTS_D...]
    all_to_all x2 -> x0, starting transfers between devices: 37.1 us -> none  [the longest x1 20.6 us: body(): lax.all_to_all(targets, 'tm', split_axis=0, concat_axis=0, tiled=True)]
  transfers between devices with their start and end apart: 2 -> 0, of which waited for: 1 -> 0; matrix products, arithmetic and copies ran while one was open for 54% -> 0% of each run, Pallas kernels for 0% -> 0%
where the time goes in v1:
time: 64.6 us; the launch traced here: 64.1 us
  Pallas kernels  55.3 us (86%)
  local copies, waits for them, and re-layouts  8.08 us (13%)
  between operations  0.69 us (1%)
    pallas_call x1, Pallas kernels, body(): pl.pallas_call(exchange_kernel, out_shape=(jax.ShapeDtypeStruct((POINTS_D...  42.3 us
    pallas_call x1, Pallas kernels, body(): pl.pallas_call(regrid_kernel, out_shape=(jax.ShapeDtypeStruct((PLANES, MA...  13.1 us
    unnamed x22, local copies, waits for them, and re-layouts  7.94 us

profile of v1, /device:TPU:1, one launch (start us, length us, event | category | flops | bytes accessed | tf_op | source)
XLA Modules:
  0.0 64.1 jit_solution(7254451532541881657)
XLA Ops:
  0.6 0.0 copy-start.2
  0.6 0.8 %copy.13 = s32[1,128,2]{2,1,0:T(8,128)S(1)} copy(s32[1,128,2]{1,2,0:T(2,128)} %param.11) | data formatting | bytes 2048 | tf_op args[1]
  1.5 0.0 copy-start.8
  1.5 0.1 reshape.9.list_ref
  1.6 0.0 copy-done.2
  1.6 0.5 copy-done.8
  2.2 0.0 copy-start
  2.2 1.1 %copy-done = bf16[2,1,384,384]{3,2,1,0:T(8,128)(2,1)S(1)} copy-done((bf16[2,1,384,384]{3,2,1,0:T(8,128)(2,1)S(1)}, bf16[2,1,384,384]{3,2,1,0:T(8,128)(2,1)}, u32[]{:S(2)}) %copy-start) | copy-done | bytes 589848
  3.2 0.0 copy-start.3
  3.2 0.8 %copy-done.3 = f32[4,32,128]{2,1,0:T(8,128)S(1)} copy-done((f32[4,32,128]{2,1,0:T(8,128)S(1)}, f32[4,32,128]{2,1,0:T(8,128)}, u32[]{:S(2)}) %copy-start.3) | copy-done | bytes 65560
  4.1 0.0 copy-start.4
  4.1 0.7 %copy-done.4 = s32[4096]{0:T(1024)S(1)} copy-done((s32[4096]{0:T(1024)S(1)}, s32[4096]{0:T(1024)}, u32[]{:S(2)}) %copy-start.4) | copy-done | bytes 16408
  4.8 0.0 copy-start.5
  4.8 0.7 %copy-done.5 = s32[4096]{0:T(1024)S(1)} copy-done((s32[4096]{0:T(1024)S(1)}, s32[4096]{0:T(1024)}, u32[]{:S(2)}) %copy-start.5) | copy-done | bytes 16408
  5.5 0.0 copy-start.6
  5.5 0.7 %copy-done.6 = s32[4096]{0:T(1024)S(1)} copy-done((s32[4096]{0:T(1024)S(1)}, s32[4096]{0:T(1024)}, u32[]{:S(2)}) %copy-start.6) | copy-done | bytes 16408
  6.2 0.0 copy-start.7
  6.2 0.7 %copy-done.7 = f32[4,8,128]{2,1,0:T(8,128)S(1)} copy-done((f32[4,8,128]{2,1,0:T(8,128)S(1)}, f32[4,8,128]{2,1,0:T(8,128)}, u32[]{:S(2)}) %copy-start.7) | copy-done | bytes 16408
  6.9 13.1 %regrid.1 = (bf16[16,9,8,128]{3,2,1,0:T(8,128)(2,1)S(1)}, f32[32,256]{1,0:T(8,128)S(1)}, f32[8,128]{1,0:T(8,128)S(1)}) custom-call(s32[256]{0:T(256)S(1)} %reshape.9.list_ref, s32[4096]{0:T(1024)S(1)} %copy-done.4, s32[4096]{0:T(1024)S(1)} %copy-done.5, s32[4096]{0:T(1024)S(1)} %copy-done.6, f32[384]{0:T(512)S(1)} %copy-done.8, ...), custom_call_target="tpu_custom_call" | custom-call | tf_op jit(solution)/shard_map/regrid/pallas_call | solution.py:333
  20.0 0.0 copy-done.1
  20.0 42.3 %exchange.1 = (bf16[32,512]{1,0:T(8,128)(2,1)S(1)}, f32[1,512]{1,0:T(1,128)S(1)}, f32[32,128]{1,0:T(8,128)S(1)}) custom-call(bf16[16,9,8,128]{3,2,1,0:T(8,128)(2,1)S(1)} %get-tuple-element.9.send_ref, f32[32,256]{1,0:T(8,128)S(1)} %get-tuple-element.10.prof_ref, f32[8,128]{1,0:T(8,128)S(1)} %get-tuple-element.11.sums_ref, bf16[512,512]{1,0:T(8,128)(2,1)S(1)} %copy-done.1), custom_call_target="tpu_custom_call" | custom-call | tf_op jit(solution)/shard_map/exchange/pallas_call | solution.py:350
  62.3 0.6 copy.17
  62.9 0.6 copy.18
  63.5 0.6 copy.19
  (1 shorter events, 0.0 us)
Async XLA Ops:
  0.6 1.0 %copy-start.2 = (bf16[128,512]{1,0:T(8,128)(2,1)S(1)}, bf16[128,512]{1,0:T(8,128)(2,1)}, u32[]{:S(2)}) copy-start(bf16[128,512]{1,0:T(8,128)(2,1)} %constant.11.clone.weights_ref) | copy-start | bytes 393220
  1.5 0.7 %copy-start.8 = (f32[384]{0:T(512)S(1)}, f32[384]{0:T(512)}, u32[]{:S(2)}) copy-start(f32[384]{0:T(512)} %constant.10.clone.stretch_ref) | copy-start | bytes 4612
  2.2 1.1 %copy-start = (bf16[2,1,384,384]{3,2,1,0:T(8,128)(2,1)S(1)}, bf16[2,1,384,384]{3,2,1,0:T(8,128)(2,1)}, u32[]{:S(2)}) copy-start(bf16[2,1,384,384]{3,2,1,0:T(8,128)(2,1)} %field_ref.1) | copy-start | bytes 1769476
  3.2 0.8 %copy-start.3 = (f32[4,32,128]{2,1,0:T(8,128)S(1)}, f32[4,32,128]{2,1,0:T(8,128)}, u32[]{:S(2)}) copy-start(f32[4,32,128]{2,1,0:T(8,128)} %constant.13.clone.mean_ref) | copy-start | bytes 196612
  4.1 0.7 %copy-start.4 = (s32[4096]{0:T(1024)S(1)}, s32[4096]{0:T(1024)}, u32[]{:S(2)}) copy-start(s32[4096]{0:T(1024)} %time_ref.1) | copy-start | bytes 49156
  4.8 0.7 %copy-start.5 = (s32[4096]{0:T(1024)S(1)}, s32[4096]{0:T(1024)}, u32[]{:S(2)}) copy-start(s32[4096]{0:T(1024)} %row_ref.1) | copy-start | bytes 49156
  5.5 0.7 %copy-start.6 = (s32[4096]{0:T(1024)S(1)}, s32[4096]{0:T(1024)}, u32[]{:S(2)}) copy-start(s32[4096]{0:T(1024)} %col_ref.1) | copy-start | bytes 49156
  6.2 0.7 %copy-start.7 = (f32[4,8,128]{2,1,0:T(8,128)S(1)}, f32[4,8,128]{2,1,0:T(8,128)}, u32[]{:S(2)}) copy-start(f32[4,8,128]{2,1,0:T(8,128)} %constant.12.clone.across_ref) | copy-start | bytes 49156
  6.9 13.1 %copy-start.1 = (bf16[512,512]{1,0:T(8,128)(2,1)S(1)}, bf16[512,512]{1,0:T(8,128)(2,1)}, u32[]{:S(2)}) copy-start(bf16[512,512]{1,0:T(8,128)(2,1)} %constant.14.clone.unsort_ref) | copy-start | bytes 1572868

commit v2 on v1

v2 whole, which is shorter than its diff:
```python
import functools
import math

import jax
import jax.numpy as jnp
import numpy as np
from jax import lax
from jax.experimental import pallas as pl
from jax.experimental.pallas import tpu as pltpu
from jax.sharding import PartitionSpec as P

PATCH, NR, NA = 128, 32, 16
HALF = PATCH // 2
SIZE = 384
POINTS_DEV = 32
OWNERS, SLOTS = 128, 2
PLANES, MATES, LEVS = 16, 8, 4
SPAN = 56
TILES = ((0, 5), (4, 7), (0, 2), (1, 7))
REACH = (48, 1)
GROUPS = 4
CHUNKS = 5
ROUND = 2
HELD = 6


def tables():
    with jax.ensure_compile_time_eval():
        cycle = jnp.arange(NR, dtype=jnp.float32)
        turn = jnp.arange(NA, dtype=jnp.float32)
        radius = (cycle[:, None] + 1.0) * (5.0 * PATCH / (16.0 * NR))
        theta = turn[None, :] * (2.0 * math.pi / NA)
        across = np.asarray((radius * jnp.cos(theta)).reshape(-1))
        along = (radius * jnp.sin(theta)).reshape(-1)
        pos = 0.5 * PATCH + along
        low = jnp.floor(pos)
        frac = pos - low
        upper = np.asarray(frac.astype(jnp.bfloat16)).astype(np.float32)
        lower = np.asarray((1.0 - frac).astype(jnp.bfloat16)).astype(np.float32)
        low = np.asarray(low.astype(jnp.int32))
        latitude = 0.25 * (0.5 * (SIZE - 1) - jnp.arange(SIZE, dtype=jnp.float32))
        stretch = np.asarray(1.0 / jnp.cos(latitude * (math.pi / 180.0)))
    turns = np.arange(NR * NA) % NA
    key = np.where(turns == NA // 4, -1e-3, np.where(turns == 3 * NA // 4, 1e-3, across))
    order = np.argsort(key, kind="stable")
    q = np.arange(NR * NA)
    weights = np.zeros((PATCH, NR * NA), np.float32)
    weights[low[order], q] += lower[order]
    weights[low[order] + 1, q] += upper[order]
    mean = np.zeros((4, NR, 128), np.float32)
    mean[q // 128, order // NA, q % 128] = 1.0 / NA
    unsort = np.zeros((NR * NA, NR * NA), np.float32)
    unsort[q, order] = 1.0
    spread = np.ascontiguousarray(np.broadcast_to(across[order].reshape(4, 1, 128), (4, 8, 128)), np.float32)
    return stretch, weights.astype(jnp.bfloat16), spread, mean, unsort.astype(jnp.bfloat16)


def merge(a, b, step, mask):
    if step == 4:
        return jnp.where(mask, a, b) + pltpu.roll(jnp.where(mask, b, a), 4, 0)
    return jnp.where(mask, a + pltpu.roll(a, 8 - step, 0), b + pltpu.roll(b, step, 0))


def kernel(
    field_hbm, list_hbm, time_hbm, row_hbm, col_hbm, stretch_hbm, weights_hbm, across_hbm, mean_hbm, unsort_hbm,
    out_ref, comp_ref, cov_ref,
    field_ref, list_ref, time_ref, row_ref, col_ref, stretch_ref, weights_ref, across_ref, mean_ref, unsort_ref, load_s,
    turned, polar, send_ref,
    planes, mates, names, named, profs, part, red1, red2, red3, mine,
    plane_s, plane_r, mate_s, mate_r, name_s, name_r, prof_s, prof_r, r1_s, r1_r, r2_s, r2_r, r3_s, r3_r,
):
    tm, lev = lax.axis_index("tm"), lax.axis_index("lev")
    z, yc = tm // MATES, lax.rem(tm, MATES)
    PER = PLANES // GROUPS

    def distance(i):
        half = (i + 1) // 2
        return lax.rem(PLANES // 2 + jnp.where(lax.rem(i, 2) == 1, half, -half), PLANES)

    def plane_peer(d):
        return {"tm": lax.rem(z + d, PLANES) * MATES + yc}

    def mate_peer(d):
        return {"tm": z * MATES + lax.rem(yc + d, MATES)}

    def lev_peer(d):
        return {"lev": lax.rem(lev + d, LEVS)}

    def copy(src, dst, s, r, peer):
        return pltpu.make_async_remote_copy(
            src_ref=src, dst_ref=dst, send_sem=s, recv_sem=r, device_id=peer, device_id_type=pl.DeviceIdType.MESH
        )

    def each(n, f):
        def step(i, c):
            f(i)
            return c

        lax.fori_loop(1, n, step, 0)

    barrier = pltpu.get_barrier_semaphore()

    def greet(peer):
        pl.semaphore_signal(barrier, inc=1, device_id=peer, device_id_type=pl.DeviceIdType.MESH)

    each(PLANES, lambda i: greet(plane_peer(distance(i - 1))))
    loads = [
        pltpu.make_async_copy(src, dst, load_s.at[i])
        for i, (src, dst) in enumerate((
            (field_hbm, field_ref), (list_hbm, list_ref), (time_hbm, time_ref), (row_hbm, row_ref), (col_hbm, col_ref),
            (stretch_hbm, stretch_ref), (weights_hbm, weights_ref), (across_hbm, across_ref), (mean_hbm, mean_ref),
            (unsort_hbm, unsort_ref),
        ))
    ]
    for load in loads:
        load.start()
    each(LEVS, lambda d: greet(lev_peer(d)))
    each(MATES, lambda d: greet(mate_peer(d)))


    def prof_copy(d):
        return copy(profs.at[0], profs.at[d], prof_s.at[d], prof_r.at[d], lev_peer(d))

    def plane_copy(i):
        d = distance(i)
        there = lax.rem(z + d, PLANES)
        return copy(send_ref.at[there], planes.at[i], plane_s.at[i], plane_r.at[i], plane_peer(d))

    def mate_copy(g, d):
        there = lax.rem(yc + d, MATES)
        return copy(
            planes.at[pl.ds(g * PER, PER), there], mates.at[d, pl.ds(g * PER, PER)],
            mate_s.at[g, d], mate_r.at[g, d], mate_peer(d),
        )

    def name_copy(d):
        return copy(names, named.at[d], name_s.at[d], name_r.at[d], mate_peer(d))

    for load in loads[:9]:
        load.wait()
    for t in range(2):
        for i in range(3):
            for j in range(3):
                tile = field_ref[t, 0, i * 128 : (i + 1) * 128, j * 128 : (j + 1) * 128]
                turned[t, i, j * 128 : (j + 1) * 128, :] = tile.astype(jnp.float32).T
    sub = lax.broadcasted_iota(jnp.int32, (8, 128), 0)
    first = (lax.broadcasted_iota(jnp.int32, (8, 128), 1) & 4) == 0
    lane = lax.broadcasted_iota(jnp.int32, (SPAN, 128), 1)
    from_start = [reach - sub.astype(jnp.float32) for reach in REACH]
    m4, m2, m1 = sub < 4, (sub & 2) == 0, (sub & 1) == 0


    def regrid(step, carry):
        total, count = carry
        halves, info = ([], []), []
        planes_now = [lax.rem(z + distance(step * ROUND + r), PLANES) for r in range(ROUND)]
        for g in planes_now:
            points = jnp.zeros((8, 128), jnp.int32)
            for o in range(MATES):
                owner = g * MATES + o
                ids = [list_ref[p, owner] for p in range(SLOTS)]
                for k in ids:
                    point = owner * POINTS_DEV + jnp.maximum(k, 0)
                    t = jnp.clip(time_ref[point] - 2 * tm, 0, 1)
                    row = jnp.clip(row_ref[point], HALF, SIZE - HALF)
                    col = jnp.clip(col_ref[point], HALF, SIZE - HALF)
                    top = row - HALF
                    b = jnp.minimum(top // 128, 1)
                    off = top - b * 128
                    for h in range(2):
                        start = col - REACH[h]
                        one = turned[t, b, pl.ds(start, SPAN), :]
                        two = turned[t, b + 1, pl.ds(start, SPAN), :]
                        halves[h].append(pltpu.roll(jnp.where(lane >= off, one, two), 128 - off, 1))
                    live = jnp.where(k >= 0, 1.0, 0.0)
                    count += live
                    info.append((stretch_ref[row], live))
                points = jnp.where(sub == o, jnp.where(first, ids[0], ids[1]), points)
            send_ref[g, MATES] = points.astype(jnp.float32).astype(jnp.bfloat16)
        mixed = [
            jnp.dot(
                jnp.concatenate(halves[h], 0).astype(jnp.bfloat16),
                weights_ref[:, h * 256 : (h + 1) * 256],
                preferred_element_type=jnp.float32,
            )
            for h in range(2)
        ]
        for o in range(ROUND * MATES):
            g = planes_now[o // MATES]
            accs = []
            for n in (2 * o, 2 * o + 1):
                for blk in range(4):
                    base = across_ref[blk] * info[n][0] + from_start[blk // 2]
                    acc = None
                    for tile in range(*TILES[blk]):
                        w = jnp.maximum(1.0 - jnp.abs(base - 8.0 * tile), 0.0)
                        at = n * SPAN + tile * 8
                        v = mixed[blk // 2][at : at + 8, (blk % 2) * 128 : (blk % 2 + 1) * 128]
                        acc = w * v if acc is None else acc + w * v
                    accs.append(acc)
            a = [accs[i] for i in (0, 4, 2, 6, 1, 5, 3, 7)]
            a = [merge(a[i], a[i + 1], 4, m4) for i in (0, 2, 4, 6)]
            a = [merge(a[i], a[i + 1], 2, m2) for i in (0, 2)]
            out = merge(a[0], a[1], 1, m1) * jnp.where(m4, info[2 * o][1], info[2 * o + 1][1])
            polar[pl.ds(pl.multiple_of((g * MATES + o % MATES) * 8, 8), 8), :] = out
            send_ref[g, o % MATES] = out.astype(jnp.bfloat16)
            total = total + out

        @pl.when(step == HELD // ROUND - 1)
        def _():
            pl.semaphore_wait(barrier, LEVS + MATES + PLANES - 3)
            for j in range(HELD):
                plane_copy(j).start()

        for r in range(ROUND):
            i = step * ROUND + r

            @pl.when(jnp.logical_and(i >= HELD, i < PLANES - 1))
            def _():
                plane_copy(i).start()

        return total, count

    total, count = lax.fori_loop(0, PLANES // ROUND, regrid, (jnp.zeros((8, 128), jnp.float32), 0.0))
    acc = jnp.zeros((NR, OWNERS * SLOTS), jnp.float32)
    for b in range(4):
        acc += lax.dot_general(
            mean_ref[b], polar[pl.ds(b, OWNERS * SLOTS, stride=4), :], (((1,), (1,)), ((), ())),
            precision=lax.Precision.HIGHEST, preferred_element_type=jnp.float32,
        )
    profs[0] = acc
    each(LEVS, lambda d: prof_copy(d).start())
    sums = jnp.where(m4, jnp.where(sub == 1, count, 0.0), total + pltpu.roll(total, 4, 0))
    planes[PLANES - 1] = send_ref[z]

    each(LEVS, lambda d: prof_copy(d).wait_recv())
    whole = jnp.concatenate([profs[lax.rem(lev - l + LEVS, LEVS)] for l in range(LEVS)], 0)
    both = lax.dot_general(
        jnp.concatenate([acc, jnp.ones((8, OWNERS * SLOTS), jnp.float32)], 0), whole, (((1,), (1,)), ((), ())),
        precision=lax.Precision.HIGHEST, preferred_element_type=jnp.float32,
    )
    for c in range(4):
        part[c] = both[c * 8 : (c + 1) * 8]
    part[4] = jnp.where(sub == 0, both[32:40], sums)

    def r1_copy(c):
        d = lax.rem(c - yc + MATES, MATES)
        return copy(part.at[c], red1.at[d], r1_s.at[c], r1_r.at[d], {"tm": z * MATES + c})

    def r2_copy(d):
        return copy(mine.at[0], red2.at[d], r2_s.at[d], r2_r.at[d], plane_peer(d))

    def r3_copy(d):
        return copy(mine.at[1], red3.at[yc], r3_s.at[d], r3_r.at[yc], mate_peer(d))

    def r1_each(f):
        for c in range(CHUNKS):
            @pl.when(yc != c)
            def _():
                f(c)

    def pass_on(g):
        for i in range(g * PER, (g + 1) * PER):
            if i < PLANES - 1:
                plane_copy(i).wait_recv()
        each(MATES, lambda d: mate_copy(g, d).start())

    r1_each(lambda c: r1_copy(c).start())
    pass_on(0)

    @pl.when(yc < CHUNKS)
    def _():
        def arrived(d):
            return copy(part.at[0], red1.at[d], r1_s.at[0], r1_r.at[d], mate_peer(1))

        each(MATES, lambda d: arrived(d).wait_recv())
        red1[0] = part[yc]
        total = red1[lax.rem(yc, MATES)]
        for m in range(1, MATES):
            total += red1[lax.rem(yc - m + MATES, MATES)]
        mine[0] = total
        each(PLANES, lambda i: r2_copy(distance(i - 1)).start())

    pass_on(1)

    @pl.when(yc < CHUNKS)
    def _():
        each(PLANES, lambda d: r2_copy(d).wait_recv())
        red2[0] = mine[0]
        total = red2[lax.rem(z, PLANES)]
        for m in range(1, PLANES):
            total += red2[lax.rem(z - m + PLANES, PLANES)]
        mine[1] = total
        red3[yc] = total
        each(MATES, lambda d: r3_copy(d).start())

    pass_on(2)
    pass_on(3)

    lane = lax.broadcasted_iota(jnp.int32, (8, 128), 1)
    ids = jnp.zeros((8, 128), jnp.float32)
    for d in range(PLANES):
        ids = jnp.where(lane // 8 == d, planes[d, MATES].astype(jnp.float32), ids)
    names[...] = ids
    each(MATES, lambda d: name_copy(d).start())

    for c in range(CHUNKS):
        @pl.when(yc != c)
        def _():
            copy(mine.at[1], red3.at[c], r3_s.at[0], r3_r.at[c], mate_peer(1)).wait_recv()

    loads[9].wait()
    count = red3[4, 1:2, :]
    every = red3[4, 0:1, :] / count
    row = lax.broadcasted_iota(jnp.int32, (NR, 128), 0)
    column = lax.broadcasted_iota(jnp.int32, (NR, 128), 1)
    own = jnp.sum(jnp.where(column == lev * NR + row, every, 0.0), axis=1, keepdims=True)
    gram = jnp.concatenate([red3[c] for c in range(4)], 0)
    cov_ref[...] = gram / count - own * every
    comp = red3[4, 4:8, :] / count
    comp = jnp.concatenate([comp[b : b + 1] for b in range(4)], 1)
    high = comp.astype(jnp.bfloat16).astype(jnp.float32)
    middle = (comp - high).astype(jnp.bfloat16).astype(jnp.float32)
    terms = jnp.concatenate([high, middle, comp - high - middle], 0).astype(jnp.bfloat16)
    terms = jnp.dot(terms, unsort_ref[...], preferred_element_type=jnp.float32)
    comp_ref[...] = terms[0:1] + terms[1:2] + terms[2:3]

    named[0] = names[...]
    mates[0] = planes[:, yc]
    line = lax.broadcasted_iota(jnp.int32, (128, 128), 0)
    lane = lax.broadcasted_iota(jnp.int32, (128, 128), 1)
    wanted = jnp.where(lane % 4 == line // POINTS_DEV, line % POINTS_DEV, -9).astype(jnp.float32)
    each(MATES, lambda d: name_copy(d).wait_recv())
    picked = jnp.zeros((128, 128), jnp.float32)
    for g in range(GROUPS):
        each(MATES, lambda d: mate_copy(g, d).wait_recv())
    for d in range(MATES):
        hit = jnp.where(wanted == named[d, pl.ds(yc, 1), :], 1.0, 0.0).astype(jnp.bfloat16)
        rows = mates[d].astype(jnp.float32).reshape(128, 128).astype(jnp.bfloat16)
        picked += jnp.dot(hit, rows, preferred_element_type=jnp.float32)
    wide = jnp.concatenate([picked[b * POINTS_DEV : (b + 1) * POINTS_DEV] for b in range(4)], 1).astype(jnp.bfloat16)
    out_ref[...] = jnp.dot(wide, unsort_ref[...], preferred_element_type=jnp.float32).astype(jnp.bfloat16)

    each(LEVS, lambda d: prof_copy(d).wait_send())
    each(PLANES, lambda i: plane_copy(i - 1).wait_send())
    each(MATES, lambda d: name_copy(d).wait_send())
    for g in range(GROUPS):
        each(MATES, lambda d: mate_copy(g, d).wait_send())
    r1_each(lambda c: r1_copy(c).wait_send())

    @pl.when(yc < CHUNKS)
    def _():
        each(PLANES, lambda d: r2_copy(d).wait_send())
        each(MATES, lambda d: r3_copy(d).wait_send())


def body(field, patch_list, track_time, track_row, track_col):
    stretch, weights, across, mean, unsort = tables()
    smem, vmem, dma = pltpu.SMEM, pltpu.VMEM, pltpu.SemaphoreType.DMA
    i32, f32, bf16 = jnp.int32, jnp.float32, jnp.bfloat16
    out, comp, cov = pl.pallas_call(
        kernel,
        out_shape=(
            jax.ShapeDtypeStruct((POINTS_DEV, NR * NA), bf16),
            jax.ShapeDtypeStruct((1, NR * NA), f32),
            jax.ShapeDtypeStruct((NR, 128), f32),
        ),
        in_specs=[pl.BlockSpec(memory_space=pl.ANY)] * 10,
        out_specs=(pl.BlockSpec(memory_space=vmem),) * 3,
        scratch_shapes=[
            vmem(field.shape, bf16), smem((SLOTS, OWNERS), i32),
            smem(track_time.shape, i32), smem(track_row.shape, i32), smem(track_col.shape, i32),
            smem(stretch.shape, f32), vmem(weights.shape, bf16), vmem(across.shape, f32), vmem(mean.shape, f32),
            vmem(unsort.shape, bf16), dma((10,)),
            vmem((2, 3, SIZE, 128), f32), vmem((OWNERS * 8, 128), f32), vmem((PLANES, MATES + 1, 8, 128), bf16),
            vmem((PLANES, MATES + 1, 8, 128), bf16), vmem((MATES, PLANES, 8, 128), bf16),
            vmem((8, 128), f32), vmem((MATES, 8, 128), f32), vmem((LEVS, NR, OWNERS * SLOTS), f32),
            vmem((CHUNKS, 8, 128), f32), vmem((MATES, 8, 128), f32), vmem((PLANES, 8, 128), f32),
            vmem((MATES, 8, 128), f32), vmem((2, 8, 128), f32),
            dma((PLANES,)), dma((PLANES,)), dma((GROUPS, MATES)), dma((GROUPS, MATES)), dma((MATES,)), dma((MATES,)),
            dma((LEVS,)), dma((LEVS,)), dma((MATES,)), dma((MATES,)), dma((PLANES,)), dma((PLANES,)),
            dma((MATES,)), dma((MATES,)),
        ],
        compiler_params=pltpu.CompilerParams(collective_id=0, has_side_effects=True, vmem_limit_bytes=60 << 20),
        name="composites",
    )(
        field, patch_list[0].T, track_time, track_row, track_col,
        jnp.asarray(stretch), jnp.asarray(weights), jnp.asarray(across), jnp.asarray(mean), jnp.asarray(unsort),
    )
    return out[:, None, :], comp, cov


def solution(mesh):
    return jax.shard_map(
        body,
        mesh=mesh,
        in_specs=(P("tm", "lev", None, None), P("tm", None, None), P(), P(), P()),
        out_specs=(P("tm", "lev", None), P("lev", None), P("lev", None)),
        check_vma=False,
    )
```

time: 64.6 us -> 49.9 us (0.77)
  Pallas kernels: 55.3 us -> 46.5 us
  local copies, waits for them, and re-layouts: 8.08 us -> 2.57 us
    pallas_call x2 -> x1, Pallas kernels: 55.3 us -> 46.5 us  [body(): pl.pallas_call(kernel, out_shape=(jax.ShapeDtypeStruct((POINTS_DEV, NR *...]
    unnamed x22 -> x7, local copies, waits for them, and re-layouts: 7.94 us -> 2.57 us
where the time goes in v2:
time: 49.9 us; the launch traced here: 49.7 us
  Pallas kernels  46.5 us (93%)
  local copies, waits for them, and re-layouts  2.57 us (5%)
  between operations  0.66 us (1%)
    pallas_call x1, Pallas kernels, body(): pl.pallas_call(kernel, out_shape=(jax.ShapeDtypeStruct((POINTS_DEV, NR *...  46.5 us
    unnamed x7, local copies, waits for them, and re-layouts  2.57 us

profile of v2, /device:TPU:1, one launch (start us, length us, event | category | flops | bytes accessed | tf_op | source)
XLA Modules:
  0.0 49.7 jit_solution(8430186357837561653)
XLA Ops:
  0.6 46.5 %composites.1 = (bf16[32,512]{1,0:T(8,128)(2,1)}, f32[1,512]{1,0:T(1,128)}, f32[32,128]{1,0:T(8,128)}) custom-call(bf16[2,1,384,384]{3,2,1,0:T(8,128)(2,1)} %field_hbm.1, s32[2,128]{1,0:T(2,128)} %bitcast.5, s32[4096]{0:T(1024)} %time_hbm.1, s32[4096]{0:T(1024)} %row_hbm.1, s32[4096]{0:T(1024)} %col_hbm.1, f32[384]{0:T(512)} %constant.10.clone.stretch_hbm, ...), custom_call_target="tpu_custom_call" | custom-call | tf_op jit(solution)/shard_map/composites/pallas_call | solution.py:361
  47.1 0.0 copy-start.1
  47.1 0.0 copy-start
  47.1 1.4 %copy.16 = bf16[32,1,512]{2,0,1:T(8,128)(2,1)} copy(bf16[32,1,512]{2,0,1:T(8,128)(2,1)} %bitcast.4) | data formatting | bytes 65536
  48.5 0.0 copy-done.1
  48.5 0.6 %copy.17 = f32[1,512]{1,0:T(1,128)} copy(f32[1,512]{1,0:T(1,128)S(1)} %copy-done.1) | data formatting | bytes 4096
  49.1 0.0 copy-done
  49.1 0.6 %copy.18 = f32[32,128]{1,0:T(8,128)} copy(f32[32,128]{1,0:T(8,128)S(1)} %copy-done) | data formatting | bytes 32768
Async XLA Ops:
  47.1 1.4 %copy-start.1 = (f32[1,512]{1,0:T(1,128)S(1)}, f32[1,512]{1,0:T(1,128)}, u32[]{:S(2)}) copy-start(f32[1,512]{1,0:T(1,128)} %get-tuple-element.13) | copy-start | bytes 6148
  47.1 2.0 %copy-start = (f32[32,128]{1,0:T(8,128)S(1)}, f32[32,128]{1,0:T(8,128)}, u32[]{:S(2)}) copy-start(f32[32,128]{1,0:T(8,128)} %get-tuple-element.14) | copy-start | bytes 49156

commit v3 on v2

--- a/solution.py
+++ b/solution.py
@@ -21,7 +21,7 @@
 GROUPS = 4
 CHUNKS = 5
 ROUND = 2
-HELD = 6
+HELD = 8
 
 
 def tables():
@@ -47,8 +47,9 @@
     weights = np.zeros((PATCH, NR * NA), np.float32)
     weights[low[order], q] += lower[order]
     weights[low[order] + 1, q] += upper[order]
-    mean = np.zeros((4, NR, 128), np.float32)
-    mean[q // 128, order // NA, q % 128] = 1.0 / NA
+    mean = np.zeros((NR, 4, 3, 128), np.float32)
+    mean[order // NA, q // 128, :, q % 128] = 1.0 / NA
+    mean = mean.reshape(NR, -1).astype(jnp.bfloat16)
     unsort = np.zeros((NR * NA, NR * NA), np.float32)
     unsort[q, order] = 1.0
     spread = np.ascontiguousarray(np.broadcast_to(across[order].reshape(4, 1, 128), (4, 8, 128)), np.float32)
@@ -222,12 +223,16 @@
         return total, count
 
     total, count = lax.fori_loop(0, PLANES // ROUND, regrid, (jnp.zeros((8, 128), jnp.float32), 0.0))
-    acc = jnp.zeros((NR, OWNERS * SLOTS), jnp.float32)
+    parts = []
     for b in range(4):
-        acc += lax.dot_general(
-            mean_ref[b], polar[pl.ds(b, OWNERS * SLOTS, stride=4), :], (((1,), (1,)), ((), ())),
-            precision=lax.Precision.HIGHEST, preferred_element_type=jnp.float32,
-        )
+        value = polar[pl.ds(b, OWNERS * SLOTS, stride=4), :]
+        for _ in range(3):
+            term = value.astype(jnp.bfloat16)
+            parts.append(term)
+            value = value - term.astype(jnp.float32)
+    acc = lax.dot_general(
+        mean_ref[...], jnp.concatenate(parts, 1), (((1,), (1,)), ((), ())), preferred_element_type=jnp.float32
+    )
     profs[0] = acc
     each(LEVS, lambda d: prof_copy(d).start())
     sums = jnp.where(m4, jnp.where(sub == 1, count, 0.0), total + pltpu.roll(total, 4, 0))
@@ -266,7 +271,6 @@
         each(MATES, lambda d: mate_copy(g, d).start())
 
     r1_each(lambda c: r1_copy(c).start())
-    pass_on(0)
 
     @pl.when(yc < CHUNKS)
     def _():
@@ -281,6 +285,7 @@
         mine[0] = total
         each(PLANES, lambda i: r2_copy(distance(i - 1)).start())
 
+    pass_on(0)
     pass_on(1)
 
     @pl.when(yc < CHUNKS)
@@ -352,6 +357,12 @@
     def _():
         each(PLANES, lambda d: r2_copy(d).wait_send())
         each(MATES, lambda d: r3_copy(d).wait_send())
+
+
+def finish_kernel(out_in, comp_in, cov_in, out_ref, comp_ref, cov_ref):
+    out_ref[...] = out_in[...]
+    comp_ref[...] = comp_in[...]
+    cov_ref[...] = cov_in[...]
 
 
 def body(field, patch_list, track_time, track_row, track_col):
@@ -370,7 +381,7 @@
         scratch_shapes=[
             vmem(field.shape, bf16), smem((SLOTS, OWNERS), i32),
             smem(track_time.shape, i32), smem(track_row.shape, i32), smem(track_col.shape, i32),
-            smem(stretch.shape, f32), vmem(weights.shape, bf16), vmem(across.shape, f32), vmem(mean.shape, f32),
+            smem(stretch.shape, f32), vmem(weights.shape, bf16), vmem(across.shape, f32), vmem(mean.shape, bf16),
             vmem(unsort.shape, bf16), dma((10,)),
             vmem((2, 3, SIZE, 128), f32), vmem((OWNERS * 8, 128), f32), vmem((PLANES, MATES + 1, 8, 128), bf16),
             vmem((PLANES, MATES + 1, 8, 128), bf16), vmem((MATES, PLANES, 8, 128), bf16),
@@ -387,6 +398,13 @@
         field, patch_list[0].T, track_time, track_row, track_col,
         jnp.asarray(stretch), jnp.asarray(weights), jnp.asarray(across), jnp.asarray(mean), jnp.asarray(unsort),
     )
+    out, comp, cov = pl.pallas_call(
+        finish_kernel,
+        out_shape=tuple(jax.ShapeDtypeStruct(a.shape, a.dtype) for a in (out, comp, cov)),
+        in_specs=[pl.BlockSpec(memory_space=vmem)] * 3,
+        out_specs=(pl.BlockSpec(memory_space=vmem),) * 3,
+        name="finish",
+    )(out, comp, cov)
     return out[:, None, :], comp, cov
 
 

time: 49.9 us -> 48.4 us (0.970)
  local copies, waits for them, and re-layouts: 2.57 us -> 0 us
  Pallas kernels: 46.5 us -> 47.6 us
    unnamed x7 -> x0, local copies, waits for them, and re-layouts: 2.57 us -> none
    pallas_call x0 -> x1, Pallas kernels: none -> 1.39 us  [body(): pl.pallas_call(finish_kernel, out_shape=tuple((jax.ShapeDtypeStruct(a.sha...]
where the time goes in v3:
time: 48.4 us; the launch traced here: 48.2 us
  Pallas kernels  47.6 us (98%)
  between operations  0.64 us (1%)
    pallas_call x1, Pallas kernels, body(): pl.pallas_call(kernel, out_shape=(jax.ShapeDtypeStruct((POINTS_DEV, NR *...  46.2 us
    pallas_call x1, Pallas kernels, body(): pl.pallas_call(finish_kernel, out_shape=tuple((jax.ShapeDtypeStruct(a.sha...  1.39 us

profile of v3, /device:TPU:1, one launch (start us, length us, event | category | flops | bytes accessed | tf_op | source)
XLA Modules:
  0.0 48.2 jit_solution(13845725952068658489)
XLA Ops:
  0.6 46.2 %composites.1 = (bf16[32,512]{1,0:T(8,128)(2,1)}, f32[1,512]{1,0:T(1,128)}, f32[32,128]{1,0:T(8,128)}) custom-call(bf16[2,1,384,384]{3,2,1,0:T(8,128)(2,1)} %field_hbm.1, s32[2,128]{1,0:T(2,128)} %bitcast.4, s32[4096]{0:T(1024)} %time_hbm.1, s32[4096]{0:T(1024)} %row_hbm.1, s32[4096]{0:T(1024)} %col_hbm.1, f32[384]{0:T(512)} %constant.10.clone.stretch_hbm, ...), custom_call_target="tpu_custom_call" | custom-call | tf_op jit(solution)/shard_map/composites/pallas_call | solution.py:372
  46.8 1.4 %finish.1 = (bf16[32,512]{1,0:T(8,128)(2,1)}, f32[1,512]{1,0:T(1,128)}, f32[32,128]{1,0:T(8,128)}) custom-call(bf16[32,512]{1,0:T(8,128)(2,1)} %get-tuple-element.9.out_in, f32[1,512]{1,0:T(1,128)} %get-tuple-element.10.comp_in, f32[32,128]{1,0:T(8,128)} %get-tuple-element.11.cov_in), custom_call_target="tpu_custom_call" | custom-call | tf_op jit(solution)/shard_map/finish/pallas_call | solution.py:401

commit v4 on v3

--- a/solution.py
+++ b/solution.py
@@ -104,7 +104,6 @@
     def greet(peer):
         pl.semaphore_signal(barrier, inc=1, device_id=peer, device_id_type=pl.DeviceIdType.MESH)
 
-    each(PLANES, lambda i: greet(plane_peer(distance(i - 1))))
     loads = [
         pltpu.make_async_copy(src, dst, load_s.at[i])
         for i, (src, dst) in enumerate((
@@ -115,6 +114,7 @@
     ]
     for load in loads:
         load.start()
+    each(PLANES, lambda i: greet(plane_peer(distance(i - 1))))
     each(LEVS, lambda d: greet(lev_peer(d)))
     each(MATES, lambda d: greet(mate_peer(d)))
 
@@ -137,13 +137,14 @@
     def name_copy(d):
         return copy(names, named.at[d], name_s.at[d], name_r.at[d], mate_peer(d))
 
-    for load in loads[:9]:
-        load.wait()
+    loads[0].wait()
     for t in range(2):
         for i in range(3):
             for j in range(3):
                 tile = field_ref[t, 0, i * 128 : (i + 1) * 128, j * 128 : (j + 1) * 128]
                 turned[t, i, j * 128 : (j + 1) * 128, :] = tile.astype(jnp.float32).T
+    for load in loads[1:9]:
+        load.wait()
     sub = lax.broadcasted_iota(jnp.int32, (8, 128), 0)
     first = (lax.broadcasted_iota(jnp.int32, (8, 128), 1) & 4) == 0
     lane = lax.broadcasted_iota(jnp.int32, (SPAN, 128), 1)

time: 48.4 us -> 47.6 us (0.983)
  Pallas kernels: 47.6 us -> 46.7 us
    pallas_call x1, Pallas kernels: 46.2 us -> 45.3 us  [body(): pl.pallas_call(kernel, out_shape=(jax.ShapeDtypeStruct((POINTS_DEV, NR *...]
where the time goes in v4:
time: 47.6 us; the launch traced here: 47.3 us
  Pallas kernels  46.7 us (98%)
  between operations  0.64 us (1%)
    pallas_call x1, Pallas kernels, body(): pl.pallas_call(kernel, out_shape=(jax.ShapeDtypeStruct((POINTS_DEV, NR *...  45.3 us
    pallas_call x1, Pallas kernels, body(): pl.pallas_call(finish_kernel, out_shape=tuple((jax.ShapeDtypeStruct(a.sha...  1.39 us

profile of v4, /device:TPU:1, one launch (start us, length us, event | category | flops | bytes accessed | tf_op | source)
XLA Modules:
  0.0 47.3 jit_solution(10546047767255647570)
XLA Ops:
  0.6 45.3 %composites.1 = (bf16[32,512]{1,0:T(8,128)(2,1)}, f32[1,512]{1,0:T(1,128)}, f32[32,128]{1,0:T(8,128)}) custom-call(bf16[2,1,384,384]{3,2,1,0:T(8,128)(2,1)} %field_hbm.1, s32[2,128]{1,0:T(2,128)} %bitcast.4, s32[4096]{0:T(1024)} %time_hbm.1, s32[4096]{0:T(1024)} %row_hbm.1, s32[4096]{0:T(1024)} %col_hbm.1, f32[384]{0:T(512)} %constant.10.clone.stretch_hbm, ...), custom_call_target="tpu_custom_call" | custom-call | tf_op jit(solution)/shard_map/composites/pallas_call | solution.py:373
  45.9 1.4 %finish.1 = (bf16[32,512]{1,0:T(8,128)(2,1)}, f32[1,512]{1,0:T(1,128)}, f32[32,128]{1,0:T(8,128)}) custom-call(bf16[32,512]{1,0:T(8,128)(2,1)} %get-tuple-element.9.out_in, f32[1,512]{1,0:T(1,128)} %get-tuple-element.10.comp_in, f32[32,128]{1,0:T(8,128)} %get-tuple-element.11.cov_in), custom_call_target="tpu_custom_call" | custom-call | tf_op jit(solution)/shard_map/finish/pallas_call | solution.py:402

commit v5 on v4

--- a/solution.py
+++ b/solution.py
@@ -20,7 +20,7 @@
 REACH = (48, 1)
 GROUPS = 4
 CHUNKS = 5
-ROUND = 2
+ROUND = 4
 HELD = 8
 
 
@@ -289,6 +289,16 @@
     pass_on(0)
     pass_on(1)
 
+    pass_on(2)
+    pass_on(3)
+
+    lane = lax.broadcasted_iota(jnp.int32, (8, 128), 1)
+    ids = jnp.zeros((8, 128), jnp.float32)
+    for d in range(PLANES):
+        ids = jnp.where(lane // 8 == d, planes[d, MATES].astype(jnp.float32), ids)
+    names[...] = ids
+    each(MATES, lambda d: name_copy(d).start())
+
     @pl.when(yc < CHUNKS)
     def _():
         each(PLANES, lambda d: r2_copy(d).wait_recv())
@@ -300,22 +310,28 @@
         red3[yc] = total
         each(MATES, lambda d: r3_copy(d).start())
 
-    pass_on(2)
-    pass_on(3)
-
-    lane = lax.broadcasted_iota(jnp.int32, (8, 128), 1)
-    ids = jnp.zeros((8, 128), jnp.float32)
-    for d in range(PLANES):
-        ids = jnp.where(lane // 8 == d, planes[d, MATES].astype(jnp.float32), ids)
-    names[...] = ids
-    each(MATES, lambda d: name_copy(d).start())
+    named[0] = names[...]
+    mates[0] = planes[:, yc]
+    line = lax.broadcasted_iota(jnp.int32, (128, 128), 0)
+    lane = lax.broadcasted_iota(jnp.int32, (128, 128), 1)
+    wanted = jnp.where(lane % 4 == line // POINTS_DEV, line % POINTS_DEV, -9).astype(jnp.float32)
+    each(MATES, lambda d: name_copy(d).wait_recv())
+    picked = jnp.zeros((128, 128), jnp.float32)
+    for g in range(GROUPS):
+        each(MATES, lambda d: mate_copy(g, d).wait_recv())
+    for d in range(MATES):
+        hit = jnp.where(wanted == named[d, pl.ds(yc, 1), :], 1.0, 0.0).astype(jnp.bfloat16)
+        rows = mates[d].astype(jnp.float32).reshape(128, 128).astype(jnp.bfloat16)
+        picked += jnp.dot(hit, rows, preferred_element_type=jnp.float32)
+    wide = jnp.concatenate([picked[b * POINTS_DEV : (b + 1) * POINTS_DEV] for b in range(4)], 1).astype(jnp.bfloat16)
+    loads[9].wait()
+    out_ref[...] = jnp.dot(wide, unsort_ref[...], preferred_element_type=jnp.float32).astype(jnp.bfloat16)
 
     for c in range(CHUNKS):
         @pl.when(yc != c)
         def _():
             copy(mine.at[1], red3.at[c], r3_s.at[0], r3_r.at[c], mate_peer(1)).wait_recv()
 
-    loads[9].wait()
     count = red3[4, 1:2, :]
     every = red3[4, 0:1, :] / count
     row = lax.broadcasted_iota(jnp.int32, (NR, 128), 0)
@@ -330,22 +346,6 @@
     terms = jnp.concatenate([high, middle, comp - high - middle], 0).astype(jnp.bfloat16)
     terms = jnp.dot(terms, unsort_ref[...], preferred_element_type=jnp.float32)
     comp_ref[...] = terms[0:1] + terms[1:2] + terms[2:3]
-
-    named[0] = names[...]
-    mates[0] = planes[:, yc]
-    line = lax.broadcasted_iota(jnp.int32, (128, 128), 0)
-    lane = lax.broadcasted_iota(jnp.int32, (128, 128), 1)
-    wanted = jnp.where(lane % 4 == line // POINTS_DEV, line % POINTS_DEV, -9).astype(jnp.float32)
-    each(MATES, lambda d: name_copy(d).wait_recv())
-    picked = jnp.zeros((128, 128), jnp.float32)
-    for g in range(GROUPS):
-        each(MATES, lambda d: mate_copy(g, d).wait_recv())
-    for d in range(MATES):
-        hit = jnp.where(wanted == named[d, pl.ds(yc, 1), :], 1.0, 0.0).astype(jnp.bfloat16)
-        rows = mates[d].astype(jnp.float32).reshape(128, 128).astype(jnp.bfloat16)
-        picked += jnp.dot(hit, rows, preferred_element_type=jnp.float32)
-    wide = jnp.concatenate([picked[b * POINTS_DEV : (b + 1) * POINTS_DEV] for b in range(4)], 1).astype(jnp.bfloat16)
-    out_ref[...] = jnp.dot(wide, unsort_ref[...], preferred_element_type=jnp.float32).astype(jnp.bfloat16)
 
     each(LEVS, lambda d: prof_copy(d).wait_send())
     each(PLANES, lambda i: plane_copy(i - 1).wait_send())

time: 47.6 us -> 45.6 us (0.958)
  Pallas kernels: 46.7 us -> 44.8 us
    pallas_call x1, Pallas kernels: 45.3 us -> 43.4 us  [body(): pl.pallas_call(kernel, out_shape=(jax.ShapeDtypeStruct((POINTS_DEV, NR *...]
where the time goes in v5:
time: 45.6 us; the launch traced here: 45.4 us
  Pallas kernels  44.8 us (98%)
  between operations  0.64 us (1%)
    pallas_call x1, Pallas kernels, body(): pl.pallas_call(kernel, out_shape=(jax.ShapeDtypeStruct((POINTS_DEV, NR *...  43.4 us
    pallas_call x1, Pallas kernels, body(): pl.pallas_call(finish_kernel, out_shape=tuple((jax.ShapeDtypeStruct(a.sha...  1.39 us

profile of v5, /device:TPU:1, one launch (start us, length us, event | category | flops | bytes accessed | tf_op | source)
XLA Modules:
  0.0 45.4 jit_solution(11702613645347899814)
XLA Ops:
  0.6 43.4 %composites.1 = (bf16[32,512]{1,0:T(8,128)(2,1)}, f32[1,512]{1,0:T(1,128)}, f32[32,128]{1,0:T(8,128)}) custom-call(bf16[2,1,384,384]{3,2,1,0:T(8,128)(2,1)} %field_hbm.1, s32[2,128]{1,0:T(2,128)} %bitcast.4, s32[4096]{0:T(1024)} %time_hbm.1, s32[4096]{0:T(1024)} %row_hbm.1, s32[4096]{0:T(1024)} %col_hbm.1, f32[384]{0:T(512)} %constant.10.clone.stretch_hbm, ...), custom_call_target="tpu_custom_call" | custom-call | tf_op jit(solution)/shard_map/composites/pallas_call | solution.py:373
  44.0 1.4 %finish.1 = (bf16[32,512]{1,0:T(8,128)(2,1)}, f32[1,512]{1,0:T(1,128)}, f32[32,128]{1,0:T(8,128)}) custom-call(bf16[32,512]{1,0:T(8,128)(2,1)} %get-tuple-element.9.out_in, f32[1,512]{1,0:T(1,128)} %get-tuple-element.10.comp_in, f32[32,128]{1,0:T(8,128)} %get-tuple-element.11.cov_in), custom_call_target="tpu_custom_call" | custom-call | tf_op jit(solution)/shard_map/finish/pallas_call | solution.py:402

commit v6 on v5

--- a/solution.py
+++ b/solution.py
@@ -20,7 +20,7 @@
 REACH = (48, 1)
 GROUPS = 4
 CHUNKS = 5
-ROUND = 4
+ROUND = 8
 HELD = 8
 
 

time: 45.6 us -> 45.1 us (0.989)
  Pallas kernels: 44.8 us -> 44.2 us
    pallas_call x1, Pallas kernels: 43.4 us -> 42.9 us  [body(): pl.pallas_call(kernel, out_shape=(jax.ShapeDtypeStruct((POINTS_DEV, NR *...]
where the time goes in v6:
time: 45.1 us; the launch traced here: 44.9 us
  Pallas kernels  44.2 us (98%)
  between operations  0.64 us (1%)
    pallas_call x1, Pallas kernels, body(): pl.pallas_call(kernel, out_shape=(jax.ShapeDtypeStruct((POINTS_DEV, NR *...  42.9 us
    pallas_call x1, Pallas kernels, body(): pl.pallas_call(finish_kernel, out_shape=tuple((jax.ShapeDtypeStruct(a.sha...  1.39 us

profile of v6, /device:TPU:1, one launch (start us, length us, event | category | flops | bytes accessed | tf_op | source)
XLA Modules:
  0.0 44.9 jit_solution(4933458969254886067)
XLA Ops:
  0.6 42.9 %composites.1 = (bf16[32,512]{1,0:T(8,128)(2,1)}, f32[1,512]{1,0:T(1,128)}, f32[32,128]{1,0:T(8,128)}) custom-call(bf16[2,1,384,384]{3,2,1,0:T(8,128)(2,1)} %field_hbm.1, s32[2,128]{1,0:T(2,128)} %bitcast.4, s32[4096]{0:T(1024)} %time_hbm.1, s32[4096]{0:T(1024)} %row_hbm.1, s32[4096]{0:T(1024)} %col_hbm.1, f32[384]{0:T(512)} %constant.10.clone.stretch_hbm, ...), custom_call_target="tpu_custom_call" | custom-call | tf_op jit(solution)/shard_map/composites/pallas_call | solution.py:373
  43.5 1.4 %finish.1 = (bf16[32,512]{1,0:T(8,128)(2,1)}, f32[1,512]{1,0:T(1,128)}, f32[32,128]{1,0:T(8,128)}) custom-call(bf16[32,512]{1,0:T(8,128)(2,1)} %get-tuple-element.9.out_in, f32[1,512]{1,0:T(1,128)} %get-tuple-element.10.comp_in, f32[32,128]{1,0:T(8,128)} %get-tuple-element.11.cov_in), custom_call_target="tpu_custom_call" | custom-call | tf_op jit(solution)/shard_map/finish/pallas_call | solution.py:402
